TPU v7x, 32 devices: a whole 2x2x4 slice. The times are simulated.
32 devices in a mesh: row: 8 (over z, y), col: 4 (over x, core).
Axes of the slice: x: 2, y: 2, z: 4, core: 2. Of those that a mesh axis runs over, the one named last changes fastest.
Arguments:
- kernel_panel: float32 [4096, 512], P('row', 'col'), may hold values from -66 to 66, as said below
- kernel_slab: float32 [4096, 2048], P('row', 'col'), may hold values from -6 to 6
Outputs:
- factor_panel: float32 [4096, 512], P('row', 'col')
- schur_slab: float32 [4096, 2048], P('row', 'col')
Inputs may be any that keep to these rules, and one draw needn't show every extreme that they name: `kernel_panel`: the first 512 rows form a symmetric positive definite matrix whose smallest eigenvalue is 0.5 or more.
All inputs are finite; a program needn't handle non-finite values.
Results may differ from a plain program's by a relative error of at most 0.00011.
Values sent between devices are 32-bit elements; how exact they have to be, the bound alone decides.
A program may use at most 64 MiB of HBM per device.

v0:
```python
import jax
import jax.numpy as jnp
from jax import lax
from jax.sharding import PartitionSpec as P


def broadcast(block, axis, owner):
    block = jnp.where(lax.axis_index(axis) == owner, block, jnp.zeros_like(block))
    return lax.psum(block, axis)


def lower_inverse(square):
    lower_factor = jnp.linalg.cholesky(square)
    identity = jnp.eye(square.shape[0], dtype=jnp.float32)
    return jax.scipy.linalg.solve_triangular(lower_factor, identity, lower=True)


def times_transpose(leading, trailing):
    return lax.dot_general(
        leading,
        trailing,
        (((1,), (1,)), ((), ())),
        precision=lax.Precision.HIGHEST,
        preferred_element_type=jnp.float32,
    )


def shards(kernel_panel, kernel_slab):
    rows_dev, block_size = kernel_panel.shape
    block_count = lax.axis_size("col")
    col_index = lax.axis_index("col")
    row_index = lax.axis_index("row")
    rows_count = lax.axis_size("row")
    span_count = kernel_slab.shape[1] // rows_dev
    global_rows = row_index * rows_dev + lax.iota(jnp.int32, rows_dev)
    panel_columns = lax.iota(jnp.int32, block_count * block_size)
    lower_mask = panel_columns[None, :] <= global_rows[:, None]
    leading_rows = broadcast(kernel_panel, "row", 0)
    whole_leading, rows_all = (
        lax.all_gather(leading_rows, "col", axis=1, tiled=True),
        lax.all_gather(kernel_panel, "col", axis=1, tiled=True),
    )
    inverse = lower_inverse(whole_leading)
    lower_rows = jnp.where(lower_mask, times_transpose(rows_all, inverse), 0.0)
    factor = lax.dynamic_slice_in_dim(lower_rows, col_index * block_size, block_size, 1)
    owner_row = 1 + (col_index * span_count + 0) % (rows_count - 1)
    gathered = broadcast(lower_rows, "row", owner_row)
    schur_out = kernel_slab - times_transpose(lower_rows, gathered)
    return (factor, schur_out)


def solution(mesh):
    placed = (P("row", "col"), P("row", "col"))
    return jax.shard_map(
        shards,
        mesh=mesh,
        in_specs=placed,
        out_specs=(P("row", "col"), P("row", "col")),
        check_vma=False,
    )
```

profile of v0, /device:TPU:3, one launch (start us, length us, event | category | flops | bytes accessed | tf_op | source)
XLA Modules:
  0.0 334.1 jit_solution(1598946369358312274)
XLA Ops:
  7.2 1.1 copy.4
  9.1 72.8 %all-reduce.4.cloned.1.call-done = f32[512,128]{0,1:T(8,128)} async-done(((f32[512,128]{0,1:T(8,128)}), f32[512,128]{0,1:T(8,128)}) %all-reduce.4.cloned.1.call-update) | async-done | bytes 262160 | tf_op jit(solution)/shard_map/psum | solution.py:9
  82.7 0.8 iota_compare_fusion
  83.7 16.9 %all-gather.3.cloned.1.call-done = f32[512,512]{0,1:T(8,128)} async-done(((f32[512,128]{0,1:T(8,128)}), f32[512,512]{0,1:T(8,128)}) %all-gather.3.cloned.1.call-update) | async-done | bytes 1048592 | tf_op jit(solution)/shard_map/all_gather | solution.py:40
  100.6 1.6 copy.5
  102.5 1.0 copy-done.1
  103.5 11.7 %cholesky.104 = f32[128,128]{1,0:T(8,128)S(1)} custom-call(f32[128,128]{1,0:T(8,128)S(1)} %cholesky.266), custom_call_target="Cholesky" | custom-call | tf_op jit(solution)/shard_map/jit(cholesky)/cholesky | solution.py:13
  115.3 9.8 %custom-call.31 = f32[1,128,128]{1,2,0:T(8,128)S(1)} custom-call(f32[1,128,128]{2,1,0:T(8,128)S(1)} %get-tuple-element.29), custom_call_target="InvertDiagBlocksLowerTriangular" | custom-call | tf_op jit(solution)/shard_map/jit(cholesky)/cholesky | solution.py:13
  125.9 11.7 %cholesky.217 = f32[128,128]{1,0:T(8,128)S(1)} custom-call(f32[128,128]{1,0:T(8,128)S(1)} %cholesky.270), custom_call_target="Cholesky" | custom-call | tf_op jit(solution)/shard_map/jit(cholesky)/cholesky | solution.py:13
  137.6 10.0 %custom-call.32 = f32[1,128,128]{1,2,0:T(8,128)S(1)} custom-call(f32[1,128,128]{2,1,0:T(8,128)S(1)} %get-tuple-element.26), custom_call_target="InvertDiagBlocksLowerTriangular" | custom-call | tf_op jit(solution)/shard_map/jit(cholesky)/cholesky | solution.py:13
  148.3 11.7 %cholesky.238 = f32[128,128]{1,0:T(8,128)S(1)} custom-call(f32[128,128]{1,0:T(8,128)S(1)} %cholesky.275), custom_call_target="Cholesky" | custom-call | tf_op jit(solution)/shard_map/jit(cholesky)/cholesky | solution.py:13
  160.7 9.8 %custom-call.33 = f32[1,128,128]{1,2,0:T(8,128)S(1)} custom-call(f32[1,128,128]{2,1,0:T(8,128)S(1)} %get-tuple-element.23), custom_call_target="InvertDiagBlocksLowerTriangular" | custom-call | tf_op jit(solution)/shard_map/jit(cholesky)/cholesky | solution.py:13
  171.1 11.7 %cholesky.255 = f32[128,128]{1,0:T(8,128)S(1)} custom-call(f32[128,128]{1,0:T(8,128)S(1)} %convolution_subtract_fusion.6), custom_call_target="Cholesky" | custom-call | tf_op jit(solution)/shard_map/jit(cholesky)/cholesky | solution.py:13
  182.8 0.9 compare_reduce_fusion
  187.1 10.1 %while.1 = (s32[]{:T(128)}, f32[512,512]{1,0:T(8,128)S(1)}, s32[4,2]{0,1:T(2,128)S(1)}, f32[4,128,128]{2,1,0:T(8,128)}, s32[]{:T(128)}) while((s32[]{:T(128)}, f32[512,512]{1,0:T(8,128)S(1)}, s32[4,2]{0,1:T(2,128)S(1)}, f32[4,128,128]{2,1,0:T(8,128)}, s32[]{:T(128)}) %tuple.32), condition=%wide.while_cond, body=%wide.while_body.sunk | while | flops 2 | bytes 132705 | solution.py:15
  187.7 1.9 bitcast_dynamic-update-slice_fusion.2
  190.2 1.9 bitcast_dynamic-update-slice_fusion.2
  192.7 1.9 bitcast_dynamic-update-slice_fusion.2
  195.2 1.9 bitcast_dynamic-update-slice_fusion.2
  197.1 40.1 %custom-call.34 = f32[4,128,128]{1,2,0:T(8,128)S(1)} custom-call(f32[4,128,128]{2,1,0:T(8,128)} %get-tuple-element.9), custom_call_target="InvertDiagBlocksLowerTriangular" | custom-call | tf_op jit(solution)/shard_map/jit(_solve_triangular)/triangular_solve | solution.py:15
  237.3 1.1 fusion.19
  241.1 4.1 %broadcast_select_fusion = (f32[512,512]{1,0:T(8,128)}, f32[512,512]{1,0:T(8,128)S(1)}) fusion(pred[]{:T(512)S(6)} %eq.19, f32[512,512]{1,0:T(8,128)} %all-gather.5.cloned.1.call-done, f32[128,512]{1,0:T(8,128)S(1)} %fusion.28, f32[128,512]{1,0:T(8,128)S(1)} %fusion.29, f32[128,512]{1,0:T(8,128)S(1)} %fusion.31, f32[128,512]{1,0:T(8,128)S(1)} %fusion.19, ...), kind=kOutput, calls=%fused_computation.34 | convolution fusion | flops 1612185600 | bytes 4196353 | tf_op jit(solution)/shard_map/dot_general | solution.py:19
  245.9 77.5 %all-reduce.6.cloned.1.call-done = f32[512,512]{1,0:T(8,128)} async-done(((f32[512,512]{1,0:T(8,128)}), f32[512,512]{1,0:T(8,128)}) %all-reduce.6.cloned.1.call-update) | async-done | bytes 1048592 | tf_op jit(solution)/shard_map/psum | solution.py:9
  323.5 4.1 %convolution_subtract_fusion = f32[512,512]{1,0:T(8,128)} fusion(f32[512,512]{1,0:T(8,128)S(1)} %copy-done.3, f32[512,512]{1,0:T(8,128)S(1)} %get-tuple-element.33, f32[512,512]{1,0:T(8,128)} %all-reduce.6.cloned.1.call-done), kind=kOutput, calls=%fused_computation.2 | convolution fusion | flops 1610874880 | bytes 4194304 | tf_op jit(solution)/shard_map/dot_general | solution.py:19
  (55 shorter events, 11.4 us)
Async XLA Ops:
  7.2 74.8 %all-reduce.4.cloned.1.call-start = ((), (), s32[]{:S(2)}) async-start(), calls=%async_computation | async-start | bytes 524288 | tf_op jit(solution)/shard_map/psum | solution.py:9
  9.1 91.6 %all-gather.3.cloned.1.call-start = ((), (), s32[]{:S(2)}) async-start(), calls=%async_computation.1 | async-start | bytes 1310720 | tf_op jit(solution)/shard_map/all_gather | solution.py:40
  81.9 159.2 %all-gather.5.cloned.1.call-start = ((), (), s32[]{:S(2)}) async-start(), calls=%async_computation.2 | async-start | bytes 1310720 | tf_op jit(solution)/shard_map/all_gather | solution.py:41
  82.7 240.8 %all-reduce.6.cloned.1.call-start = ((), (), s32[]{:S(2)}) async-start(), calls=%async_computation.3 | async-start | bytes 2097152 | tf_op jit(solution)/shard_map/psum | solution.py:9
  100.6 1.7 copy-start
  102.5 1.0 copy-start.1
  103.5 21.7 %copy-start.2 = (f32[512,512]{1,0:T(8,128)S(1)}, f32[512,512]{1,0:T(8,128)}, u32[]{:S(2)}) copy-start(f32[512,512]{1,0:T(8,128)} %copy-done.1) | copy-start | bytes 3145732
  245.2 78.3 %copy-start.3 = (f32[512,512]{1,0:T(8,128)S(1)}, f32[512,512]{1,0:T(8,128)}, u32[]{:S(2)}) copy-start(f32[512,512]{1,0:T(8,128)} %param.3) | copy-start | bytes 3145732
Sparse Core Ops, SparseCore 0:
  11.9 69.9 all-reduce.3
  83.6 17.0 all-gather.2
  102.3 16.9 all-gather.4
  245.3 78.1 all-reduce.5
where the time goes:
time: 337 us; the launch traced here: 334 us
  waiting for transfers between devices  168 us (50%)
  other arithmetic  121 us (36%)
  between operations  16.6 us (5%)
  local copies, waits for them, and re-layouts  14.6 us (4%)
  matrix products  13.8 us (4%)
    psum x2, waiting for transfers between devices, broadcast(): return lax.psum(block, axis)  150 us
    another operation x14, other arithmetic, lower_inverse(): lower_factor = jnp.linalg.cholesky(square)  78.8 us
    another operation x3, other arithmetic, lower_inverse(): return jax.scipy.linalg.solve_triangular(lower_factor, identity, lower=True)  40.3 us
    all_gather x1, waiting for transfers between devices, shards(): lax.all_gather(leading_rows, 'col', axis=1, tiled=True)  16.9 us
    another operation x12, local copies, waits for them, and re-layouts  10 us
    dot_general x2, matrix products, times_transpose(): lax.dot_general(leading, trailing, (((1,), (1,)), ((), ())), precision=la...  8.12 us
  transfers between devices with their start and end apart: 4, of which 3 were waited for; matrix products, arithmetic and copies ran while one was open for 41% of the time, Pallas kernels for 0%

commit v1 on v0

v1 whole, which is shorter than its diff:
```python
import functools

import jax
import jax.numpy as jnp
from jax import lax
from jax.experimental import pallas as pl
from jax.experimental.pallas import tpu as pltpu
from jax.sharding import PartitionSpec as P

F32, BF16 = jnp.float32, jnp.bfloat16
SUB = 8
MID = 32


def split(x):
    high = x.astype(BF16)
    return high, (x - high.astype(F32)).astype(BF16)


def dot(a, b, dims):
    return lax.dot_general(a, b, (dims, ((), ())), preferred_element_type=F32)


def dot3(a, b, dims=((1,), (1,))):
    (ah, al), (bh, bl) = a, b
    return dot(ah, bh, dims) + (dot(ah, bl, dims) + dot(al, bh, dims))


def sublane(x, j):
    return jnp.broadcast_to(x[j : j + 1, :], x.shape)


def lane(x, j):
    return jnp.broadcast_to(x[:, j : j + 1], x.shape)


def newton_reciprocal(d):
    r = pl.reciprocal(d, approx=True)
    r = r * (2.0 - d * r)
    return r * (2.0 - d * r)


def lower_inverse(square, hook):
    n = square.shape[0]
    count = n // SUB
    row_ids = lax.broadcasted_iota(jnp.int32, (SUB, n), 0)
    lane_ids = lax.broadcasted_iota(jnp.int32, (SUB, n), 1)
    work = [square[SUB * i : SUB * (i + 1)] for i in range(count)]
    unit = [jnp.where(lane_ids == row_ids + SUB * i, 1.0, 0.0).astype(F32) for i in range(count)]
    per = MID // SUB
    for b in range(n // MID):
        last = per * (b + 1)
        for t in range(per * b, last):
            cols = {i: [lane(work[i], SUB * t + j) for j in range(SUB)] for i in range(t, last)}
            pivots = jnp.ones((SUB, n), F32)
            for j in range(SUB):
                pivot = sublane(cols[t][j], j)
                inverse = newton_reciprocal(pivot)
                pivots = jnp.where(row_ids == j, pivot, pivots)
                work_row, unit_row = sublane(work[t], j), sublane(unit[t], j)
                heads = {k: sublane(cols[t][k], j) for k in range(j + 1, SUB)}
                for i in range(t, last):
                    column = cols[i][j]
                    if i == t:
                        column = jnp.where(row_ids > j, column, 0.0)
                    factor = column * inverse
                    for k in range(j + 1, SUB):
                        cols[i][k] = cols[i][k] - factor * heads[k]
                    work[i] = work[i] - factor * work_row
                    unit[i] = unit[i] - factor * unit_row
            scale = lax.rsqrt(pivots)
            scale = scale * (1.5 - 0.5 * pivots * scale * scale)
            work[t] = work[t] * scale
            unit[t] = unit[t] * scale
        if last < count:
            rows = jnp.concatenate(work[per * b : last], axis=0)
            both = jnp.concatenate([rows, jnp.concatenate(unit[per * b : last], axis=0)], axis=1)
            rh, rl = split(rows)
            bh, bl = split(both)
            left = jnp.concatenate([rh, rh, rl], axis=0)
            right = jnp.concatenate([bh, bl, bh], axis=0)
            update = dot(left, right, ((0,), (0,)))
            for i in range(last, count):
                work[i] = work[i] - update[SUB * i : SUB * (i + 1), :n]
                unit[i] = unit[i] - update[SUB * i : SUB * (i + 1), n:]
        hook()
    return jnp.concatenate(unit, axis=0)


def kernel(rows_count, cols_count, panel, slab, factor_out, schur_out,
           lead, rows, far, low_h, low_l, own_h, own_l, far_h, far_l,
           lead_recv, rows_recv, far_recv, lead_down, lead_cross, lead_sib, lead_par,
           rows_sib, rows_par, far_up, far_down, far_cross):
    r, c = lax.axis_index("row"), lax.axis_index("col")
    size, width = panel.shape
    chunks = cols_count
    step = size // chunks
    core = c % 2
    sibling = c + 1 - 2 * core
    partner = r + 1 - 2 * (r % 2)
    pairs = cols_count // 2
    root = 1 + c % (rows_count - 1)
    on_chain = (root % 2) == (r % 2)

    def to(row, col):
        return {"row": row, "col": col}

    def peer(i):
        return 2 * ((c // 2 + i + 1) % pairs) + core

    barrier = pltpu.get_barrier_semaphore()

    def greet(row, col):
        pl.semaphore_signal(barrier, inc=1, device_id=to(row, col), device_id_type=pl.DeviceIdType.MESH)

    greet(r, sibling)
    for i in range(pairs - 1):
        greet(r, peer(i))
    greet(partner, c)
    has_up, has_down = r >= 2, r + 2 < rows_count

    @pl.when(has_up)
    def _():
        greet(r - 2, c)

    @pl.when(has_down)
    def _():
        greet(r + 2, c)

    rows[c] = panel[...]

    @pl.when(r == 0)
    def _():
        lead[c] = panel[...]

    pl.semaphore_wait(barrier, 1 + pairs + has_up.astype(jnp.int32) + has_down.astype(jnp.int32))

    def copy(src, dst, send, recv, row, col):
        return pltpu.make_async_remote_copy(src_ref=src, dst_ref=dst, send_sem=send, recv_sem=recv,
                                            device_id=to(row, col), device_id_type=pl.DeviceIdType.MESH)

    def lead_copy(block, q, send, row, col):
        part = lead.at[block, pl.ds(q * step, step), :]
        return copy(part, part, send, lead_recv.at[block, q], row, col)

    def rows_copy(block, send, col):
        return copy(rows.at[block], rows.at[block], send, rows_recv.at[block], r, col)

    def far_copy(block, send, row):
        return copy(far.at[block], far.at[block], send, far_recv.at[block], row, c)

    def lead_arrived(block, q):
        lead_copy(block, q, lead_down.at[0], r, sibling).wait_recv()

    def rows_arrived(block):
        rows_copy(block, rows_par.at[0], sibling).wait_recv()

    def far_arrived(block):
        far_copy(block, far_up.at[0], partner).wait_recv()

    for q in range(chunks):
        @pl.when(r > 0)
        def _():
            lead_arrived(c, q)

        @pl.when(has_down)
        def _():
            lead_copy(c, q, lead_down.at[q], r + 2, c).start()

        @pl.when(r == 0)
        def _():
            lead_copy(c, q, lead_cross.at[q], 1, c).start()

        for i in range(pairs - 1):
            lead_copy(c, q, lead_par.at[i, q], r, peer(i)).start()
        lead_copy(c, q, lead_sib.at[0, q], r, sibling).start()
    for i in range(pairs - 1):
        rows_copy(c, rows_par.at[i], peer(i)).start()
    rows_copy(c, rows_sib.at[0], sibling).start()
    for q in range(chunks):
        for i in range(pairs - 1):
            lead_arrived(peer(i), q)
            lead_copy(peer(i), q, lead_sib.at[i + 1, q], r, sibling).start()

    def rows_ready(block):
        @pl.when(block % 2 != core)
        def _():
            rows_arrived(block)

    reach = (rows_count + 1) // 2
    distance = jnp.abs(root - r) // 2
    hooks = cols_count + reach
    state = {"point": 0, "next": 0}

    def forward(m):
        q = m - distance

        @pl.when(on_chain & (q >= 0) & (q < cols_count))
        def _():
            @pl.when(r == root)
            def _():
                @pl.when(q % 2 != core)
                def _():
                    rows_arrived(q)

                far[q] = rows[q]

            @pl.when(r != root)
            def _():
                far_arrived(q)

            @pl.when((r <= root) & has_up)
            def _():
                far_copy(q, far_up.at[q], r - 2).start()

            @pl.when((r >= root) & has_down)
            def _():
                far_copy(q, far_down.at[q], r + 2).start()

            far_copy(q, far_cross.at[q], partner).start()

    def hook():
        state["point"] += 1
        if state["point"] == 1:
            for i in range(pairs - 1):
                rows_arrived(peer(i))
                rows_copy(peer(i), rows_sib.at[i + 1], sibling).start()
        elif state["point"] % 2 == 0 and state["next"] < hooks:
            forward(state["next"])
            state["next"] += 1

    lane_ids = lax.broadcasted_iota(jnp.int32, (size, width), 1)
    row_ids = lax.broadcasted_iota(jnp.int32, (size, width), 0)

    def solve(block, k, source, high, low, inverse, top):
        done = k * width
        value = source[k, top:, :]
        if k:
            value = value - dot3((high[top:, :done], low[top:, :done]),
                                 (low_h[done : done + width, :done], low_l[done : done + width, :done]))
        return dot3(split(value), inverse)

    def keep(x, k, high, low, top):
        xh, xl = split(x)
        high[top:, k * width : (k + 1) * width] = xh
        low[top:, k * width : (k + 1) * width] = xl

    inverses = []
    for k in range(cols_count):
        @pl.when(k % 2 != core)
        def _():
            for q in range(chunks):
                lead_arrived(k, q)

        first, end = k * width, (k + 1) * width
        square = lead[k, first:end, :]
        if k:
            square = square - dot3((low_h[first:end, :first], low_l[first:end, :first]),
                                   (low_h[first:end, :first], low_l[first:end, :first]))
        inverse = split(lower_inverse(square, hook))
        inverses.append(inverse)
        if k + 1 < cols_count:
            keep(solve(None, k, lead, low_h, low_l, inverse, end), k, low_h, low_l, end)

    for k in range(cols_count):
        @pl.when((r != root) & (k % 2 != core))
        def _():
            rows_arrived(k)

        x = solve(None, k, rows, own_h, own_l, inverses[k], 0)
        x = jnp.where(k * width + lane_ids <= r * size + row_ids, x, 0.0)
        keep(x, k, own_h, own_l, 0)

        @pl.when(c == k)
        def _():
            factor_out[...] = x

    if state["next"] < hooks:
        def rest(m, carry):
            forward(m)
            return carry

        lax.fori_loop(state["next"], hooks, rest, 0)
    for k in range(cols_count):
        @pl.when(jnp.logical_not(on_chain))
        def _():
            far_arrived(k)

        x = solve(None, k, far, far_h, far_l, inverses[k], 0)
        x = jnp.where(k * width + lane_ids <= root * size + row_ids, x, 0.0)
        keep(x, k, far_h, far_l, 0)
    schur_out[...] = slab[...] - dot3((own_h[...], own_l[...]), (far_h[...], far_l[...]))

    for q in range(chunks):
        @pl.when(has_down)
        def _():
            lead_copy(c, q, lead_down.at[q], r + 2, c).wait_send()

        @pl.when(r == 0)
        def _():
            lead_copy(c, q, lead_cross.at[q], 1, c).wait_send()

        for i in range(pairs - 1):
            lead_copy(c, q, lead_par.at[i, q], r, peer(i)).wait_send()
            lead_copy(peer(i), q, lead_sib.at[i + 1, q], r, sibling).wait_send()
        lead_copy(c, q, lead_sib.at[0, q], r, sibling).wait_send()
    rows_copy(c, rows_sib.at[0], sibling).wait_send()
    for i in range(pairs - 1):
        rows_copy(c, rows_par.at[i], peer(i)).wait_send()
        rows_copy(peer(i), rows_sib.at[i + 1], sibling).wait_send()

    @pl.when(on_chain)
    def _():
        for q in range(cols_count):
            @pl.when((r <= root) & has_up)
            def _():
                far_copy(q, far_up.at[q], r - 2).wait_send()

            @pl.when((r >= root) & has_down)
            def _():
                far_copy(q, far_down.at[q], r + 2).wait_send()

            far_copy(q, far_cross.at[q], partner).wait_send()


def shards(rows_count, cols_count, panel, slab):
    size, width = panel.shape
    whole = cols_count * width
    pairs = cols_count // 2
    dma = pltpu.SemaphoreType.DMA
    block = pltpu.VMEM((cols_count, size, width), F32)
    half = pltpu.VMEM((size, whole), BF16)
    vmem = pl.BlockSpec(memory_space=pltpu.VMEM)
    return pl.pallas_call(
        functools.partial(kernel, rows_count, cols_count),
        out_shape=(jax.ShapeDtypeStruct(panel.shape, F32), jax.ShapeDtypeStruct(slab.shape, F32)),
        in_specs=[vmem, vmem],
        out_specs=(vmem, vmem),
        scratch_shapes=[
            block, block, block, half, half, half, half, half, half,
            dma((cols_count, cols_count)), dma((cols_count,)), dma((cols_count,)),
            dma((cols_count,)), dma((cols_count,)), dma((pairs, cols_count)), dma((pairs, cols_count)),
            dma((pairs,)), dma((pairs,)),
            dma((cols_count,)), dma((cols_count,)), dma((cols_count,)),
        ],
        compiler_params=pltpu.CompilerParams(
            collective_id=0, has_side_effects=True, vmem_limit_bytes=48 * 1024 * 1024
        ),
    )(panel, slab)


def solution(mesh):
    placed = (P("row", "col"), P("row", "col"))
    return jax.shard_map(
        functools.partial(shards, mesh.shape["row"], mesh.shape["col"]),
        mesh=mesh,
        in_specs=placed,
        out_specs=placed,
        check_vma=False,
    )
```

time: 337 us -> 58 us (0.17)
  waiting for transfers between devices: 168 us -> 0 us
  other arithmetic: 121 us -> 0 us
  Pallas kernels: 0 us -> 53.3 us
  between operations: 16.6 us -> 0.65 us
  matrix products: 13.8 us -> 0 us
  local copies, waits for them, and re-layouts: 14.6 us -> 3.84 us
    psum x2 -> x0, waiting for transfers between devices: 150 us -> none  [broadcast(): return lax.psum(block, axis)]
    another operation x17 -> x0, other arithmetic: 119 us -> none  [the longest x14 78.8 us: lower_inverse(): lower_factor = jnp.linalg.cholesky(square)]
    pallas_call x0 -> x1, Pallas kernels: none -> 53.3 us  [shards(): pl.pallas_call(functools.partial(kernel, rows_count, cols_count), out_sha...]
    all_gather x2 -> x0, waiting for transfers between devices: 17 us -> none  [the longest x1 16.9 us: shards(): lax.all_gather(leading_rows, 'col', axis=1, tiled=True)]
    another operation x17 -> x0, local copies, waits for them, and re-layouts: 10.2 us -> none
    dot_general x2 -> x0, matrix products: 8.12 us -> none  [times_transpose(): lax.dot_general(leading, trailing, (((1,), (1,)), ((), ())), precision=la...]
    another operation x13 -> x0, matrix products: 5.64 us -> none  [the longest x7 3.77 us: lower_inverse(): return jax.scipy.linalg.solve_triangular(lower_factor, identity, lower=True)]
  transfers between devices with their start and end apart: 4 -> 0, of which waited for: 3 -> 0; matrix products, arithmetic and copies ran while one was open for 41% -> 0% of each run, Pallas kernels for 0% -> 0%
where the time goes in v1:
time: 58 us; the launch traced here: 57.8 us
  Pallas kernels  53.3 us (92%)
  local copies, waits for them, and re-layouts  3.84 us (7%)
  between operations  0.65 us (1%)
    pallas_call x1, Pallas kernels, shards(): pl.pallas_call(functools.partial(kernel, rows_count, cols_count), out_sha...  53.3 us
    unnamed x6, local copies, waits for them, and re-layouts  3.84 us

profile of v1, /device:TPU:3, one launch (start us, length us, event | category | flops | bytes accessed | tf_op | source)
XLA Modules:
  0.0 57.8 jit_solution(10465206861757196118)
XLA Ops:
  0.6 0.0 copy-start
  0.6 1.2 %copy-done = f32[512,512]{1,0:T(8,128)S(1)} copy-done((f32[512,512]{1,0:T(8,128)S(1)}, f32[512,512]{1,0:T(8,128)}, u32[]{:S(2)}) %copy-start) | copy-done | bytes 1048600
  1.9 0.0 copy-start.1
  1.9 0.9 %copy-done.1 = f32[512,128]{1,0:T(8,128)S(1)} copy-done((f32[512,128]{1,0:T(8,128)S(1)}, f32[512,128]{1,0:T(8,128)}, u32[]{:S(2)}) %copy-start.1) | copy-done | bytes 262168
  2.8 53.3 %shard_map.41 = (f32[512,128]{1,0:T(8,128)S(1)}, f32[512,512]{1,0:T(8,128)S(1)}) custom-call(f32[512,128]{1,0:T(8,128)S(1)} %copy-done.1, f32[512,512]{1,0:T(8,128)S(1)} %copy-done), custom_call_target="tpu_custom_call" | custom-call | tf_op jit(solution)/shard_map/pallas_call | solution.py:334
  56.2 0.7 %copy.6 = f32[512,128]{1,0:T(8,128)} copy(f32[512,128]{1,0:T(8,128)S(1)} %get-tuple-element.4) | data formatting | bytes 524288
  56.9 1.0 %copy.7 = f32[512,512]{1,0:T(8,128)} copy(f32[512,512]{1,0:T(8,128)S(1)} %get-tuple-element.5) | data formatting | bytes 2097152
Async XLA Ops:
  0.6 1.2 %copy-start = (f32[512,512]{1,0:T(8,128)S(1)}, f32[512,512]{1,0:T(8,128)}, u32[]{:S(2)}) copy-start(f32[512,512]{1,0:T(8,128)} %slab.1) | copy-start | bytes 3145732
  1.9 0.9 %copy-start.1 = (f32[512,128]{1,0:T(8,128)S(1)}, f32[512,128]{1,0:T(8,128)}, u32[]{:S(2)}) copy-start(f32[512,128]{1,0:T(8,128)} %panel.1) | copy-start | bytes 786436

commit v2 on v1

--- a/solution.py
+++ b/solution.py
@@ -34,10 +34,9 @@
     return jnp.broadcast_to(x[:, j : j + 1], x.shape)
 
 
-def newton_reciprocal(d):
-    r = pl.reciprocal(d, approx=True)
-    r = r * (2.0 - d * r)
-    return r * (2.0 - d * r)
+def inverse_root(p):
+    s = lax.rsqrt(p)
+    return s * (1.5 - 0.5 * p * s * s)
 
 
 def lower_inverse(square, hook):
@@ -52,26 +51,42 @@
         last = per * (b + 1)
         for t in range(per * b, last):
             cols = {i: [lane(work[i], SUB * t + j) for j in range(SUB)] for i in range(t, last)}
-            pivots = jnp.ones((SUB, n), F32)
-            for j in range(SUB):
-                pivot = sublane(cols[t][j], j)
-                inverse = newton_reciprocal(pivot)
-                pivots = jnp.where(row_ids == j, pivot, pivots)
-                work_row, unit_row = sublane(work[t], j), sublane(unit[t], j)
-                heads = {k: sublane(cols[t][k], j) for k in range(j + 1, SUB)}
+            d1s = jnp.ones((SUB, n), F32); d2s = d1s; es = jnp.zeros((SUB, n), F32)
+            for j in range(0, SUB, 2):
+                top, nxt = cols[t][j], cols[t][j + 1]
+                d1, e, d2 = sublane(top, j), sublane(nxt, j), sublane(nxt, j + 1)
+                det = d1 * d2 - e * e
+                inv = pl.reciprocal(det, approx=True)
+                first, second = row_ids == j, row_ids == j + 1
+                d1s = jnp.where(first | second, d1, d1s)
+                es = jnp.where(second, e, es)
+                d2s = jnp.where(second, d2, d2s)
+                def mixed(x):
+                    h1, h2 = sublane(x, j), sublane(x, j + 1)
+                    return h1 * d2 - h2 * e, h2 * d1 - h1 * e
+                heads = {k: mixed(cols[t][k]) for k in range(j + 2, SUB)}
+                wg, ug = mixed(work[t]), mixed(unit[t])
                 for i in range(t, last):
-                    column = cols[i][j]
+                    c1, c2 = cols[i][j], cols[i][j + 1]
                     if i == t:
-                        column = jnp.where(row_ids > j, column, 0.0)
-                    factor = column * inverse
-                    for k in range(j + 1, SUB):
-                        cols[i][k] = cols[i][k] - factor * heads[k]
-                    work[i] = work[i] - factor * work_row
-                    unit[i] = unit[i] - factor * unit_row
-            scale = lax.rsqrt(pivots)
-            scale = scale * (1.5 - 0.5 * pivots * scale * scale)
-            work[t] = work[t] * scale
-            unit[t] = unit[t] * scale
+                        below = row_ids > j + 1
+                        c1, c2 = jnp.where(below, c1, 0.0), jnp.where(below, c2, 0.0)
+                    for k in range(j + 2, SUB):
+                        g1, g2 = heads[k]
+                        cols[i][k] = cols[i][k] - (c1 * g1 + c2 * g2) * inv
+                    work[i] = work[i] - (c1 * wg[0] + c2 * wg[1]) * inv
+                    unit[i] = unit[i] - (c1 * ug[0] + c2 * ug[1]) * inv
+            odd = row_ids % 2 == 1
+            r1 = pl.reciprocal(d1s, approx=True)
+            r1 = r1 * (2.0 - d1s * r1)
+            slope = es * r1
+            pivots = jnp.where(odd, d2s - es * slope, d1s)
+            scale = inverse_root(pivots)
+            def finish(x):
+                up = jnp.concatenate([x[:1], x[:-1]], axis=0)
+                return (x - slope * up) * scale
+            work[t] = finish(work[t])
+            unit[t] = finish(unit[t])
         if last < count:
             rows = jnp.concatenate(work[per * b : last], axis=0)
             both = jnp.concatenate([rows, jnp.concatenate(unit[per * b : last], axis=0)], axis=1)
@@ -88,7 +103,7 @@
 
 
 def kernel(rows_count, cols_count, panel, slab, factor_out, schur_out,
-           lead, rows, far, low_h, low_l, own_h, own_l, far_h, far_l,
+           lead, rows, far, slab_in, local_sem, low_h, low_l, own_h, own_l, far_h, far_l,
            lead_recv, rows_recv, far_recv, lead_down, lead_cross, lead_sib, lead_par,
            rows_sib, rows_par, far_up, far_down, far_cross):
     r, c = lax.axis_index("row"), lax.axis_index("col")
@@ -127,12 +142,16 @@
     def _():
         greet(r + 2, c)
 
-    rows[c] = panel[...]
+    panel_copy = pltpu.make_async_copy(panel, rows.at[c], local_sem.at[0])
+    lead_own = pltpu.make_async_copy(panel, lead.at[c], local_sem.at[1])
+    slab_copy = pltpu.make_async_copy(slab, slab_in, local_sem.at[2])
 
     @pl.when(r == 0)
     def _():
-        lead[c] = panel[...]
-
+        lead_own.start()
+
+    panel_copy.start()
+    slab_copy.start()
     pl.semaphore_wait(barrier, 1 + pairs + has_up.astype(jnp.int32) + has_down.astype(jnp.int32))
 
     def copy(src, dst, send, recv, row, col):
@@ -158,34 +177,42 @@
     def far_arrived(block):
         far_copy(block, far_up.at[0], partner).wait_recv()
 
+    @pl.when(r == 0)
+    def _():
+        lead_own.wait()
+
     for q in range(chunks):
-        @pl.when(r > 0)
-        def _():
-            lead_arrived(c, q)
-
-        @pl.when(has_down)
-        def _():
-            lead_copy(c, q, lead_down.at[q], r + 2, c).start()
-
-        @pl.when(r == 0)
-        def _():
-            lead_copy(c, q, lead_cross.at[q], 1, c).start()
-
-        for i in range(pairs - 1):
-            lead_copy(c, q, lead_par.at[i, q], r, peer(i)).start()
-        lead_copy(c, q, lead_sib.at[0, q], r, sibling).start()
+        @pl.when(c <= q)
+        def _():
+            @pl.when(r > 0)
+            def _():
+                lead_arrived(c, q)
+
+            @pl.when(has_down)
+            def _():
+                lead_copy(c, q, lead_down.at[q], r + 2, c).start()
+
+            @pl.when(r == 0)
+            def _():
+                lead_copy(c, q, lead_cross.at[q], 1, c).start()
+
+            for i in range(pairs - 1):
+                lead_copy(c, q, lead_par.at[i, q], r, peer(i)).start()
+            lead_copy(c, q, lead_sib.at[0, q], r, sibling).start()
+    panel_copy.wait()
     for i in range(pairs - 1):
         rows_copy(c, rows_par.at[i], peer(i)).start()
     rows_copy(c, rows_sib.at[0], sibling).start()
-    for q in range(chunks):
+
+    def pass_on(first):
         for i in range(pairs - 1):
-            lead_arrived(peer(i), q)
-            lead_copy(peer(i), q, lead_sib.at[i + 1, q], r, sibling).start()
-
-    def rows_ready(block):
-        @pl.when(block % 2 != core)
-        def _():
-            rows_arrived(block)
+            for q in range(chunks):
+                @pl.when(((peer(i) == 0) == first) & (peer(i) <= q))
+                def _():
+                    lead_arrived(peer(i), q)
+                    lead_copy(peer(i), q, lead_sib.at[i + 1, q], r, sibling).start()
+
+    pass_on(True)
 
     reach = (rows_count + 1) // 2
     distance = jnp.abs(root - r) // 2
@@ -219,13 +246,21 @@
 
             far_copy(q, far_cross.at[q], partner).start()
 
-    def hook():
+    points = width // MID
+
+    def hook(k):
         state["point"] += 1
+        if k and state["point"] % points == 1:
+            own_rows_ready(k - 1)
+        if k and state["point"] % points == 2:
+            own_rows(k - 1)
         if state["point"] == 1:
+            pass_on(False)
+        elif state["point"] == 2:
             for i in range(pairs - 1):
                 rows_arrived(peer(i))
                 rows_copy(peer(i), rows_sib.at[i + 1], sibling).start()
-        elif state["point"] % 2 == 0 and state["next"] < hooks:
+        elif state["point"] % 2 == 1 and state["next"] < hooks:
             forward(state["next"])
             state["next"] += 1
 
@@ -245,11 +280,25 @@
         high[top:, k * width : (k + 1) * width] = xh
         low[top:, k * width : (k + 1) * width] = xl
 
+    def own_rows_ready(k):
+        @pl.when((r != root) & (k % 2 != core))
+        def _():
+            rows_arrived(k)
+
+    def own_rows(k):
+        x = solve(None, k, rows, own_h, own_l, inverses[k], 0)
+        x = jnp.where(k * width + lane_ids <= r * size + row_ids, x, 0.0)
+        keep(x, k, own_h, own_l, 0)
+
+        @pl.when(c == k)
+        def _():
+            factor_out[...] = x
+
     inverses = []
     for k in range(cols_count):
         @pl.when(k % 2 != core)
         def _():
-            for q in range(chunks):
+            for q in range(k, chunks):
                 lead_arrived(k, q)
 
         first, end = k * width, (k + 1) * width
@@ -257,24 +306,13 @@
         if k:
             square = square - dot3((low_h[first:end, :first], low_l[first:end, :first]),
                                    (low_h[first:end, :first], low_l[first:end, :first]))
-        inverse = split(lower_inverse(square, hook))
+        inverse = split(lower_inverse(square, functools.partial(hook, k)))
         inverses.append(inverse)
         if k + 1 < cols_count:
             keep(solve(None, k, lead, low_h, low_l, inverse, end), k, low_h, low_l, end)
 
-    for k in range(cols_count):
-        @pl.when((r != root) & (k % 2 != core))
-        def _():
-            rows_arrived(k)
-
-        x = solve(None, k, rows, own_h, own_l, inverses[k], 0)
-        x = jnp.where(k * width + lane_ids <= r * size + row_ids, x, 0.0)
-        keep(x, k, own_h, own_l, 0)
-
-        @pl.when(c == k)
-        def _():
-            factor_out[...] = x
-
+    own_rows_ready(cols_count - 1)
+    own_rows(cols_count - 1)
     if state["next"] < hooks:
         def rest(m, carry):
             forward(m)
@@ -289,21 +327,28 @@
         x = solve(None, k, far, far_h, far_l, inverses[k], 0)
         x = jnp.where(k * width + lane_ids <= root * size + row_ids, x, 0.0)
         keep(x, k, far_h, far_l, 0)
-    schur_out[...] = slab[...] - dot3((own_h[...], own_l[...]), (far_h[...], far_l[...]))
+    slab_copy.wait()
+    schur_out[...] = slab_in[...] - dot3((own_h[...], own_l[...]), (far_h[...], far_l[...]))
 
     for q in range(chunks):
-        @pl.when(has_down)
-        def _():
-            lead_copy(c, q, lead_down.at[q], r + 2, c).wait_send()
-
-        @pl.when(r == 0)
-        def _():
-            lead_copy(c, q, lead_cross.at[q], 1, c).wait_send()
+        @pl.when(c <= q)
+        def _():
+            @pl.when(has_down)
+            def _():
+                lead_copy(c, q, lead_down.at[q], r + 2, c).wait_send()
+
+            @pl.when(r == 0)
+            def _():
+                lead_copy(c, q, lead_cross.at[q], 1, c).wait_send()
+
+            for i in range(pairs - 1):
+                lead_copy(c, q, lead_par.at[i, q], r, peer(i)).wait_send()
+            lead_copy(c, q, lead_sib.at[0, q], r, sibling).wait_send()
 
         for i in range(pairs - 1):
-            lead_copy(c, q, lead_par.at[i, q], r, peer(i)).wait_send()
-            lead_copy(peer(i), q, lead_sib.at[i + 1, q], r, sibling).wait_send()
-        lead_copy(c, q, lead_sib.at[0, q], r, sibling).wait_send()
+            @pl.when(peer(i) <= q)
+            def _():
+                lead_copy(peer(i), q, lead_sib.at[i + 1, q], r, sibling).wait_send()
     rows_copy(c, rows_sib.at[0], sibling).wait_send()
     for i in range(pairs - 1):
         rows_copy(c, rows_par.at[i], peer(i)).wait_send()
@@ -330,21 +375,21 @@
     dma = pltpu.SemaphoreType.DMA
     block = pltpu.VMEM((cols_count, size, width), F32)
     half = pltpu.VMEM((size, whole), BF16)
-    vmem = pl.BlockSpec(memory_space=pltpu.VMEM)
+    vmem, hbm = pl.BlockSpec(memory_space=pltpu.VMEM), pl.BlockSpec(memory_space=pltpu.HBM)
     return pl.pallas_call(
         functools.partial(kernel, rows_count, cols_count),
         out_shape=(jax.ShapeDtypeStruct(panel.shape, F32), jax.ShapeDtypeStruct(slab.shape, F32)),
-        in_specs=[vmem, vmem],
+        in_specs=[hbm, hbm],
         out_specs=(vmem, vmem),
         scratch_shapes=[
-            block, block, block, half, half, half, half, half, half,
+            block, block, block, pltpu.VMEM(slab.shape, F32), dma((3,)), half, half, half, half, half, half,
             dma((cols_count, cols_count)), dma((cols_count,)), dma((cols_count,)),
             dma((cols_count,)), dma((cols_count,)), dma((pairs, cols_count)), dma((pairs, cols_count)),
             dma((pairs,)), dma((pairs,)),
             dma((cols_count,)), dma((cols_count,)), dma((cols_count,)),
         ],
         compiler_params=pltpu.CompilerParams(
-            collective_id=0, has_side_effects=True, vmem_limit_bytes=48 * 1024 * 1024
+            collective_id=0, has_side_effects=True, vmem_limit_bytes=63 * 1024 * 1024
         ),
     )(panel, slab)
 

time: 58 us -> 54.4 us (0.938)
  Pallas kernels: 53.3 us -> 49.6 us
    pallas_call x1, Pallas kernels: 53.3 us -> 49.6 us  [shards(): pl.pallas_call(functools.partial(kernel, rows_count, cols_count), out_sha...]
    unnamed x6 -> x2, local copies, waits for them, and re-layouts: 3.84 us -> 3.93 us
where the time goes in v2:
time: 54.4 us; the launch traced here: 54.2 us
  Pallas kernels  49.6 us (91%)
  local copies, waits for them, and re-layouts  3.93 us (7%)
  between operations  0.64 us (1%)
    pallas_call x1, Pallas kernels, shards(): pl.pallas_call(functools.partial(kernel, rows_count, cols_count), out_sha...  49.6 us
    unnamed x2, local copies, waits for them, and re-layouts  3.93 us

profile of v2, /device:TPU:3, one launch (start us, length us, event | category | flops | bytes accessed | tf_op | source)
XLA Modules:
  0.0 54.2 jit_solution(5059400926502626978)
XLA Ops:
  0.6 49.6 %shard_map.41 = (f32[512,128]{1,0:T(8,128)}, f32[512,512]{1,0:T(8,128)}) custom-call(f32[512,128]{1,0:T(8,128)} %panel.1, f32[512,512]{1,0:T(8,128)} %slab.1), custom_call_target="tpu_custom_call" | custom-call | tf_op jit(solution)/shard_map/pallas_call | solution.py:379
  50.2 1.7 %copy.6 = f32[512,128]{1,0:T(8,128)} copy(f32[512,128]{1,0:T(8,128)} %get-tuple-element.4) | data formatting | bytes 524288
  51.9 2.3 %copy.7 = f32[512,512]{1,0:T(8,128)} copy(f32[512,512]{1,0:T(8,128)} %get-tuple-element.5) | data formatting | bytes 2097152

commit v3 on v2

--- a/solution.py
+++ b/solution.py
@@ -181,6 +181,22 @@
     def _():
         lead_own.wait()
 
+    panel_copy.wait()
+
+    def send_rows():
+        for i in range(pairs - 1):
+            rows_copy(c, rows_par.at[i], peer(i)).start()
+        rows_copy(c, rows_sib.at[0], sibling).start()
+
+    def pass_rows():
+        for i in range(pairs - 1):
+            rows_arrived(peer(i))
+            rows_copy(peer(i), rows_sib.at[i + 1], sibling).start()
+
+    @pl.when(r > 0)
+    def _():
+        send_rows()
+
     for q in range(chunks):
         @pl.when(c <= q)
         def _():
@@ -199,10 +215,9 @@
             for i in range(pairs - 1):
                 lead_copy(c, q, lead_par.at[i, q], r, peer(i)).start()
             lead_copy(c, q, lead_sib.at[0, q], r, sibling).start()
-    panel_copy.wait()
-    for i in range(pairs - 1):
-        rows_copy(c, rows_par.at[i], peer(i)).start()
-    rows_copy(c, rows_sib.at[0], sibling).start()
+    @pl.when(r == 0)
+    def _():
+        send_rows()
 
     def pass_on(first):
         for i in range(pairs - 1):
@@ -217,34 +232,43 @@
     reach = (rows_count + 1) // 2
     distance = jnp.abs(root - r) // 2
     hooks = cols_count + reach
+
+    def turn(o):
+        return 2 * ((c // 2 + o // 2) % pairs) + (core + o) % 2
+
+    def far_send(q):
+        @pl.when((r <= root) & has_up)
+        def _():
+            far_copy(q, far_up.at[q], r - 2).start()
+
+        @pl.when((r >= root) & has_down)
+        def _():
+            far_copy(q, far_down.at[q], r + 2).start()
+
+        far_copy(q, far_cross.at[q], partner).start()
+
     state = {"point": 0, "next": 0}
 
     def forward(m):
-        q = m - distance
-
-        @pl.when(on_chain & (q >= 0) & (q < cols_count))
-        def _():
-            @pl.when(r == root)
-            def _():
-                @pl.when(q % 2 != core)
-                def _():
-                    rows_arrived(q)
-
-                far[q] = rows[q]
-
-            @pl.when(r != root)
-            def _():
-                far_arrived(q)
-
-            @pl.when((r <= root) & has_up)
-            def _():
-                far_copy(q, far_up.at[q], r - 2).start()
-
-            @pl.when((r >= root) & has_down)
-            def _():
-                far_copy(q, far_down.at[q], r + 2).start()
-
-            far_copy(q, far_cross.at[q], partner).start()
+        o = m + 1 - distance
+
+        @pl.when(on_chain & (r != root) & (o >= 0) & (o < cols_count))
+        def _():
+            far_arrived(turn(o))
+            far_send(turn(o))
+
+    @pl.when(r > 0)
+    def _():
+        pass_rows()
+
+    @pl.when(r == root)
+    def _():
+        for o in range(cols_count):
+            q = turn(o)
+            if o % 2:
+                rows_arrived(q)
+            far[q] = rows[q]
+            far_send(q)
 
     points = width // MID
 
@@ -257,9 +281,9 @@
         if state["point"] == 1:
             pass_on(False)
         elif state["point"] == 2:
-            for i in range(pairs - 1):
-                rows_arrived(peer(i))
-                rows_copy(peer(i), rows_sib.at[i + 1], sibling).start()
+            @pl.when(r == 0)
+            def _():
+                pass_rows()
         elif state["point"] % 2 == 1 and state["next"] < hooks:
             forward(state["next"])
             state["next"] += 1
@@ -389,7 +413,7 @@
             dma((cols_count,)), dma((cols_count,)), dma((cols_count,)),
         ],
         compiler_params=pltpu.CompilerParams(
-            collective_id=0, has_side_effects=True, vmem_limit_bytes=63 * 1024 * 1024
+            collective_id=0, has_side_effects=True, vmem_limit_bytes=48 * 1024 * 1024
         ),
     )(panel, slab)
 

time: 54.4 us -> 47.5 us (0.87)
  the two profiles are of different devices: /device:TPU:3 before, /device:TPU:30 now
where the time goes in v3:
time: 47.5 us; the launch traced here: 47.3 us
  Pallas kernels  42.8 us (90%)
  local copies, waits for them, and re-layouts  3.84 us (8%)
  between operations  0.65 us (1%)
    pallas_call x1, Pallas kernels, shards(): pl.pallas_call(functools.partial(kernel, rows_count, cols_count), out_sha...  42.8 us
    unnamed x6, local copies, waits for them, and re-layouts  3.84 us

profile of v3, /device:TPU:30, one launch (start us, length us, event | category | flops | bytes accessed | tf_op | source)
XLA Modules:
  0.0 47.3 jit_solution(14982885431656943842)
XLA Ops:
  0.6 0.0 copy-start
  0.6 1.2 %copy-done = f32[512,512]{1,0:T(8,128)S(1)} copy-done((f32[512,512]{1,0:T(8,128)S(1)}, f32[512,512]{1,0:T(8,128)}, u32[]{:S(2)}) %copy-start) | copy-done | bytes 1048600
  1.9 0.0 copy-start.1
  1.9 0.9 %copy-done.1 = f32[512,128]{1,0:T(8,128)S(1)} copy-done((f32[512,128]{1,0:T(8,128)S(1)}, f32[512,128]{1,0:T(8,128)}, u32[]{:S(2)}) %copy-start.1) | copy-done | bytes 262168
  2.8 42.8 %shard_map.41 = (f32[512,128]{1,0:T(8,128)S(1)}, f32[512,512]{1,0:T(8,128)S(1)}) custom-call(f32[512,128]{1,0:T(8,128)S(1)} %copy-done.1, f32[512,512]{1,0:T(8,128)S(1)} %copy-done), custom_call_target="tpu_custom_call" | custom-call | tf_op jit(solution)/shard_map/pallas_call | solution.py:403
  45.6 0.7 %copy.6 = f32[512,128]{1,0:T(8,128)} copy(f32[512,128]{1,0:T(8,128)S(1)} %get-tuple-element.4) | data formatting | bytes 524288
  46.3 1.0 %copy.7 = f32[512,512]{1,0:T(8,128)} copy(f32[512,512]{1,0:T(8,128)S(1)} %get-tuple-element.5) | data formatting | bytes 2097152
Async XLA Ops:
  0.6 1.2 %copy-start = (f32[512,512]{1,0:T(8,128)S(1)}, f32[512,512]{1,0:T(8,128)}, u32[]{:S(2)}) copy-start(f32[512,512]{1,0:T(8,128)} %slab.1) | copy-start | bytes 3145732
  1.9 0.9 %copy-start.1 = (f32[512,128]{1,0:T(8,128)S(1)}, f32[512,128]{1,0:T(8,128)}, u32[]{:S(2)}) copy-start(f32[512,128]{1,0:T(8,128)} %panel.1) | copy-start | bytes 786436
